TPU v7x, 128 devices: a whole 4x4x4 slice. The times are simulated.
128 devices in a mesh: dp: 16 (over z, y), ctx: 8 (over x, core).
Axes of the slice: x: 4, y: 4, z: 4, core: 2. Of those that a mesh axis runs over, the one named last changes fastest.
Arguments:
- tokens: bfloat16 [16384, 2048], P(('dp', 'ctx')), may hold values from -6 to 6
- cotangent: bfloat16 [16384, 2048], P(('dp', 'ctx')), may hold values from -6 to 6
- lengths: int32 [16, 4], P('dp'), may hold values from 0 to 1024, as said below
- spans: int32 [16, 8, 2], P('dp'), may hold values from 0 to 15, as said below
- gain_attn: bfloat16 [2048], P(('dp', 'ctx')), may hold values from 0.25 to 1.75
- w_query: bfloat16 [2048, 2048], P(('dp', 'ctx')), may hold values from -0.125 to 0.125
- w_key: bfloat16 [2048, 256], P(('dp', 'ctx')), may hold values from -0.125 to 0.125
- w_value: bfloat16 [2048, 256], P(('dp', 'ctx')), may hold values from -0.125 to 0.125
- w_out: bfloat16 [2048, 2048], P(('dp', 'ctx')), may hold values from -1.5 to 1.5
- gain_mlp: bfloat16 [2048], P(('dp', 'ctx')), may hold values from 0.25 to 1.75
- w_gate: bfloat16 [2048, 5632], P(('dp', 'ctx')), may hold values from -0.125 to 0.125
- w_up: bfloat16 [2048, 5632], P(('dp', 'ctx')), may hold values from -0.125 to 0.125
- w_down: bfloat16 [5632, 2048], P(('dp', 'ctx')), may hold values from -0.078125 to 0.078125
Outputs:
- block_out: bfloat16 [16384, 2048], P(('dp', 'ctx'))
- input_grad: float32 [16384, 2048], P(('dp', 'ctx'))
- grad_gain_attn: float32 [2048], P(('dp', 'ctx'))
- grad_query: float32 [2048, 2048], P(('dp', 'ctx'))
- grad_key: float32 [2048, 256], P(('dp', 'ctx'))
- grad_value: float32 [2048, 256], P(('dp', 'ctx'))
- grad_out: float32 [2048, 2048], P(('dp', 'ctx'))
- grad_gain_mlp: float32 [2048], P(('dp', 'ctx'))
- grad_gate: float32 [2048, 5632], P(('dp', 'ctx'))
- grad_up: float32 [2048, 5632], P(('dp', 'ctx'))
- grad_down: float32 [5632, 2048], P(('dp', 'ctx'))
Inputs may be any that keep to these rules, and one draw needn't show every extreme that they name: Row g holds the lengths of group g's 4 packed sequences, which fill its 1024 places in order; the first or the last of them is 512 or longer, and some group holds one sequence of 1024. A group's 1024 places form 16 blocks of 64 in order; index r of ctx holds block spans[g, r, 0], of the first half, then block spans[g, r, 1], of the second half; each block is held once.
All inputs are finite; a program needn't handle non-finite values.
Results may differ from a plain program's by a relative error of at most 0.017.
Values may be sent and summed in bfloat16 or wider, within the bound.
A program may use at most 448 MiB of HBM per device.

v0:
```python
import jax
import jax.numpy as jnp
from jax import lax
from jax.sharding import PartitionSpec as P

D = 2048
HEADS = 32
KV_HEADS = 4
HEAD_DIM = 64


EPSILON = 1e-05
NEG_LARGE = -1e30
ACROSS = (((1,), (1,)), ((), ()))
DOWNWARD = (((0,), (0,)), ((), ()))


def rope_tables(position):
    inverse = jnp.power(
        jnp.float32(10000.0), -jnp.arange(0, HEAD_DIM, 2).astype(jnp.float32) / HEAD_DIM
    )
    angles = position.astype(jnp.float32)[:, None] * inverse[None, :]
    return (jnp.cos(angles)[:, None, :], jnp.sin(angles)[:, None, :])


def rotate(values, cos_table, sin_table):
    half_dim = values.shape[-1] // 2
    leading = values[..., :half_dim]
    trailing = values[..., half_dim:]
    return jnp.concatenate(
        [leading * cos_table - trailing * sin_table, trailing * cos_table + leading * sin_table], -1
    )


def rms_scale(values):
    return lax.rsqrt(jnp.mean(values * values, -1, keepdims=True) + EPSILON)


def norm_back(values, scale_rows, scaled):
    return scale_rows * scaled - values * scale_rows * scale_rows * scale_rows * jnp.mean(
        scaled * values, -1, keepdims=True
    )


def contract(left_op, right_op, dims_pair):
    return lax.dot_general(left_op, right_op, dims_pair, preferred_element_type=jnp.float32)


def per_device(
    tokens,
    cotangent,
    lengths,
    spans,
    gain_attn,
    w_query,
    w_key,
    w_value,
    w_out,
    gain_mlp,
    w_gate,
    w_up,
    w_down,
):
    tok_rows = tokens.shape[0]
    ctx_count = lax.axis_size("ctx")
    ctx_rank = lax.axis_index("ctx")
    group_rows = tok_rows * ctx_count
    span_len = tok_rows // 2
    kv_groups = HEADS // KV_HEADS
    kv_width = w_key.shape[1]
    score_scale = HEAD_DIM ** (-0.5)
    row_ids = jnp.arange(group_rows, dtype=jnp.int32)
    slot_ids = jnp.arange(2 * ctx_count, dtype=jnp.int32)
    table = spans.reshape(-1)
    span_ids = jnp.sum(
        jnp.where((row_ids // span_len)[:, None] == slot_ids[None, :], table[None, :], 0), 1
    )
    packed = span_ids * span_len + row_ids % span_len
    length_row = lengths[0]
    seq_ends = jnp.cumsum(length_row)
    before = seq_ends[None, :] <= packed[:, None]
    doc_ids = jnp.sum(before.astype(jnp.int32), 1)
    position = packed - jnp.sum(jnp.where(before, length_row[None, :], 0), 1)
    local_start = ctx_rank * tok_rows
    own_packed = lax.dynamic_slice_in_dim(packed, local_start, tok_rows)
    own_docs = lax.dynamic_slice_in_dim(doc_ids, local_start, tok_rows)
    own_position = lax.dynamic_slice_in_dim(position, local_start, tok_rows)
    allowed = (own_docs[:, None] == doc_ids[None, :]) & (packed[None, :] <= own_packed[:, None])
    cos_table, sin_table = rope_tables(own_position)
    tokens_f = tokens.astype(jnp.float32)
    scale_attn = rms_scale(tokens_f)
    gain_piece = lax.all_gather(gain_attn, ("dp", "ctx"), axis=0, tiled=True)
    query_piece = lax.all_gather(w_query, ("dp", "ctx"), axis=0, tiled=True)
    key_piece = lax.all_gather(w_key, ("dp", "ctx"), axis=0, tiled=True)
    value_piece = lax.all_gather(w_value, ("dp", "ctx"), axis=0, tiled=True)
    columns = tokens_f
    normed_piece = (columns * scale_attn * gain_piece.astype(jnp.float32)[None, :]).astype(
        jnp.bfloat16
    )
    query_sum = jnp.dot(normed_piece, query_piece, preferred_element_type=jnp.float32)
    key_sum = jnp.dot(normed_piece, key_piece, preferred_element_type=jnp.float32)
    value_sum = jnp.dot(normed_piece, value_piece, preferred_element_type=jnp.float32)
    normed = normed_piece
    query_rot = rotate(query_sum.reshape(tok_rows, HEADS, HEAD_DIM), cos_table, sin_table).astype(
        jnp.bfloat16
    )
    key_rot = rotate(key_sum.reshape(tok_rows, KV_HEADS, HEAD_DIM), cos_table, sin_table).astype(
        jnp.bfloat16
    )
    value_low = value_sum.reshape(tok_rows, KV_HEADS, HEAD_DIM).astype(jnp.bfloat16)
    key_group, value_group = (
        lax.all_gather(key_rot, "ctx", axis=0, tiled=True),
        lax.all_gather(value_low, "ctx", axis=0, tiled=True),
    )
    query_groups = query_rot.reshape(tok_rows, KV_HEADS, kv_groups, HEAD_DIM)

    def scores_of():
        raw_scores = (
            jnp.einsum(
                "qkgd,nkd->kgqn", query_groups, key_group, preferred_element_type=jnp.float32
            )
            * score_scale
        )
        return jnp.where(allowed[None, None], raw_scores, NEG_LARGE)

    scores = scores_of()
    peak = jnp.max(scores, -1, keepdims=True)
    expo = jnp.exp(scores - peak)
    denom = jnp.sum(expo, -1, keepdims=True)
    log_total = peak + jnp.log(denom)
    probs_low = (expo / denom).astype(jnp.bfloat16)
    attended = jnp.einsum(
        "kgqn,nkd->qkgd", probs_low, value_group, preferred_element_type=jnp.float32
    ).reshape(tok_rows, D)
    attended_low = attended.astype(jnp.bfloat16)
    columns = attended_low
    branch = jnp.dot(
        columns,
        lax.all_gather(w_out, ("dp", "ctx"), axis=0, tiled=True),
        preferred_element_type=jnp.float32,
    )
    hidden = tokens_f + branch
    scale_mlp = rms_scale(hidden)
    gain_full, gate_full, up_full, down_full = (
        lax.all_gather(gain_mlp, ("dp", "ctx"), axis=0, tiled=True),
        lax.all_gather(w_gate, ("dp", "ctx"), axis=0, tiled=True),
        lax.all_gather(w_up, ("dp", "ctx"), axis=0, tiled=True),
        lax.all_gather(w_down, ("dp", "ctx"), axis=0, tiled=True),
    )
    normed_mlp = (hidden * scale_mlp * gain_full.astype(jnp.float32)[None, :]).astype(jnp.bfloat16)
    gate_act = jnp.dot(normed_mlp, gate_full, preferred_element_type=jnp.float32)
    up_act = jnp.dot(normed_mlp, up_full, preferred_element_type=jnp.float32)
    gate_sig = jax.nn.sigmoid(gate_act)
    silu_act = gate_act * gate_sig
    inner_low = (silu_act * up_act).astype(jnp.bfloat16)
    block_out = hidden + jnp.dot(inner_low, down_full, preferred_element_type=jnp.float32)
    gain_full, gate_full, up_full, down_full = (
        lax.all_gather(gain_mlp, ("dp", "ctx"), axis=0, tiled=True),
        lax.all_gather(w_gate, ("dp", "ctx"), axis=0, tiled=True),
        lax.all_gather(w_up, ("dp", "ctx"), axis=0, tiled=True),
        lax.all_gather(w_down, ("dp", "ctx"), axis=0, tiled=True),
    )
    cot_f = cotangent.astype(jnp.float32)
    inner_grad = contract(cotangent, down_full, ACROSS)
    gate_grad = (inner_grad * up_act * gate_sig * (1.0 + gate_act * (1.0 - gate_sig))).astype(
        jnp.bfloat16
    )
    up_grad = (inner_grad * silu_act).astype(jnp.bfloat16)
    normed_grad = contract(gate_grad, gate_full, ACROSS) + contract(up_grad, up_full, ACROSS)
    scaled_mlp = normed_grad * gain_full.astype(jnp.float32)[None, :]
    hidden_grad = cot_f + norm_back(hidden, scale_mlp, scaled_mlp)
    gain_mlp_term = jnp.sum(normed_grad * hidden * scale_mlp, 0)
    both_grads = jnp.concatenate([gate_grad, up_grad], 1)
    ff_width = w_gate.shape[1]
    rows_part = inner_low
    grad_down = lax.psum_scatter(
        contract(rows_part, cotangent, DOWNWARD), ("dp", "ctx"), scatter_dimension=0, tiled=True
    )
    rows_part = normed_mlp
    mlp_sum = lax.psum_scatter(
        contract(rows_part, both_grads, DOWNWARD), ("dp", "ctx"), scatter_dimension=0, tiled=True
    )
    grad_gate = mlp_sum[:, :ff_width]
    grad_up = mlp_sum[:, ff_width:]
    branch_grad = hidden_grad.astype(jnp.bfloat16)
    attended_grad = contract(
        branch_grad, lax.all_gather(w_out, ("dp", "ctx"), axis=0, tiled=True), ACROSS
    )
    out_term = contract(attended_low, branch_grad, DOWNWARD)
    grad_heads = attended_grad.astype(jnp.bfloat16).reshape(tok_rows, KV_HEADS, kv_groups, HEAD_DIM)
    probs = jnp.exp(scores_of() - log_total)
    probs_low = probs.astype(jnp.bfloat16)
    prob_grad = jnp.einsum(
        "qkgd,nkd->kgqn", grad_heads, value_group, preferred_element_type=jnp.float32
    )
    delta = jnp.sum(probs * prob_grad, -1, keepdims=True)
    score_grad = (probs * (prob_grad - delta)).astype(jnp.bfloat16)
    query_grad = (
        jnp.einsum("kgqn,nkd->qkgd", score_grad, key_group, preferred_element_type=jnp.float32)
        * score_scale
    )
    key_terms = (
        jnp.einsum("kgqn,qkgd->nkd", score_grad, query_groups, preferred_element_type=jnp.float32)
        * score_scale
    )
    value_terms = jnp.einsum(
        "kgqn,qkgd->nkd", probs_low, grad_heads, preferred_element_type=jnp.float32
    )
    key_own, value_own = (
        lax.psum_scatter(
            key_terms.astype(jnp.bfloat16), "ctx", scatter_dimension=0, tiled=True
        ).astype(jnp.float32),
        lax.psum_scatter(
            value_terms.astype(jnp.bfloat16), "ctx", scatter_dimension=0, tiled=True
        ).astype(jnp.float32),
    )
    query_low = (
        rotate(query_grad.reshape(tok_rows, HEADS, HEAD_DIM), cos_table, -sin_table)
        .reshape(tok_rows, D)
        .astype(jnp.bfloat16)
    )
    key_low = (
        rotate(key_own, cos_table, -sin_table).reshape(tok_rows, kv_width).astype(jnp.bfloat16)
    )
    value_grad = value_own.reshape(tok_rows, kv_width).astype(jnp.bfloat16)
    gain_piece, query_piece, key_piece, value_piece = lax.all_gather(
        (gain_attn, w_query, w_key, w_value), ("dp", "ctx"), axis=0, tiled=True
    )
    normed_piece = (
        contract(query_low, query_piece, ACROSS)
        + contract(key_low, key_piece, ACROSS)
        + contract(value_grad, value_piece, ACROSS)
    )
    stacked = jnp.stack([normed_piece * gain_piece.astype(jnp.float32)[None, :], normed_piece])
    input_grad = hidden_grad + norm_back(tokens_f, scale_attn, stacked[0])
    gain_attn_term = jnp.sum(stacked[1] * tokens_f * scale_attn, 0)
    query_term = contract(normed, query_low, DOWNWARD)
    key_term = contract(normed, key_low, DOWNWARD)
    value_term = contract(normed, value_grad, DOWNWARD)
    summed = (
        lax.psum_scatter(gain_attn_term, ("dp", "ctx"), scatter_dimension=0, tiled=True),
        lax.psum_scatter(gain_mlp_term, ("dp", "ctx"), scatter_dimension=0, tiled=True),
        lax.psum_scatter(query_term, ("dp", "ctx"), scatter_dimension=0, tiled=True),
        lax.psum_scatter(key_term, ("dp", "ctx"), scatter_dimension=0, tiled=True),
        lax.psum_scatter(value_term, ("dp", "ctx"), scatter_dimension=0, tiled=True),
        lax.psum_scatter(out_term, ("dp", "ctx"), scatter_dimension=0, tiled=True),
    )
    return (
        block_out.astype(jnp.bfloat16),
        input_grad,
        summed[0],
        summed[2],
        summed[3],
        summed[4],
        summed[5],
        summed[1],
        grad_gate,
        grad_up,
        grad_down,
    )


def solution(mesh):
    in_specs = (
        P(("dp", "ctx"), None),
        P(("dp", "ctx"), None),
        P("dp", None),
        P("dp", None, None),
        P(("dp", "ctx")),
        P(("dp", "ctx"), None),
        P(("dp", "ctx"), None),
        P(("dp", "ctx"), None),
        P(("dp", "ctx"), None),
        P(("dp", "ctx")),
        P(("dp", "ctx"), None),
        P(("dp", "ctx"), None),
        P(("dp", "ctx"), None),
    )
    out_specs = (
        P(("dp", "ctx"), None),
        P(("dp", "ctx"), None),
        P(("dp", "ctx")),
        P(("dp", "ctx"), None),
        P(("dp", "ctx"), None),
        P(("dp", "ctx"), None),
        P(("dp", "ctx"), None),
        P(("dp", "ctx")),
        P(("dp", "ctx"), None),
        P(("dp", "ctx"), None),
        P(("dp", "ctx"), None),
    )
    return jax.shard_map(
        per_device, mesh=mesh, in_specs=in_specs, out_specs=out_specs, check_vma=False
    )
```

profile of v0, /device:TPU:0, one launch (start us, length us, event | category | flops | bytes accessed | tf_op | source)
XLA Modules:
  0.0 4250.1 jit_solution(1356141093315356060)
XLA Ops:
  15.3 68.8 %all-reduce.7 = (bf16[2048]{0:T(1024)(128)(2,1)S(1)}, bf16[2048]{0:T(1024)(128)(2,1)S(1)}) all-reduce(bf16[2048]{0:T(1024)(128)(2,1)S(1)} %dynamic-update-slice, bf16[2048]{0:T(1024)(128)(2,1)S(1)} %dynamic-update-slice.1), channel_id=1, replica_groups=mesh['dp'=16,'ctx'=8] {'dp','ctx'}, use_global_device_ids=true, to_apply=%add | all-reduce | flops 4096 | bytes 16384
  87.6 1.7 convolution_convert_fusion.1
  89.5 51.3 %all-gather.11.cloned.1.call-done = bf16[2048,256]{1,0:T(8,128)(2,1)} async-done(((bf16[16,256]{1,0:T(8,128)(2,1)}), bf16[2048,256]{1,0:T(8,128)(2,1)}) %all-gather.11.cloned.1.call-update) | async-done | bytes 1048592 | tf_op jit(solution)/shard_map/all_gather | solution.py:94
  140.7 2.0 fusion.67
  142.7 12.2 all_gather.46
  155.0 13.4 all_gather.44
  168.4 43.0 %all-gather.13.cloned.1.call-done = bf16[2048,2048]{1,0:T(8,128)(2,1)} async-done(((bf16[16,2048]{1,0:T(8,128)(2,1)}), bf16[2048,2048]{1,0:T(8,128)(2,1)}) %all-gather.13.cloned.1.call-update) | async-done | bytes 8388624 | tf_op jit(solution)/shard_map/all_gather | solution.py:93
  211.4 7.0 fusion.65
  218.6 7.2 fusion.71
  225.8 8.3 fusion.4
  234.1 7.5 fusion.24
  241.6 40.4 all-gather.15.cloned.1.call-done
  281.9 4.7 multiply_reduce_fusion.2
  286.9 88.7 %all-gather.21.cloned.1.call-done = bf16[128,44,2048]{2,1,0:T(8,128)(2,1)} async-done(((bf16[1,44,2048]{2,1,0:T(8,128)(2,1)}), bf16[128,44,2048]{2,1,0:T(8,128)(2,1)}) %all-gather.21.cloned.1.call-update) | async-done | bytes 23068688 | tf_op jit(solution)/shard_map/all_gather | solution.py:148
  375.6 30.7 reshape.290
  406.3 61.5 %all-gather.19.cloned.1.call-done = bf16[2048,5632]{1,0:T(8,128)(2,1)} async-done(((bf16[16,5632]{1,0:T(8,128)(2,1)}), bf16[2048,5632]{1,0:T(8,128)(2,1)}) %all-gather.19.cloned.1.call-update) | async-done | bytes 23068688 | tf_op jit(solution)/shard_map/all_gather | solution.py:147
  467.8 12.3 fusion.73
  480.1 80.0 %all-gather.17.cloned.1.call-done = bf16[2048,5632]{1,0:T(8,128)(2,1)} async-done(((bf16[16,5632]{1,0:T(8,128)(2,1)}), bf16[2048,5632]{1,0:T(8,128)(2,1)}) %all-gather.17.cloned.1.call-update) | async-done | bytes 23068688 | tf_op jit(solution)/shard_map/all_gather | solution.py:146
  560.1 12.3 fusion.72
  572.4 15.0 multiply_convert_fusion
  587.5 13.4 fusion.74
  600.9 14.1 multiply_reduce_fusion
  615.0 1.6 subtract_add_fusion
  616.6 7.1 convolution_convert_fusion
  624.9 9.3 fusion.20
  634.2 10.7 fusion.1
  645.0 2.1 copy.84
  647.1 11.8 fusion.3
  659.0 3.3 copy-done
  662.3 3.4 fusion.23
  665.7 2.0 copy.82
  667.8 33.9 fusion.10
  702.8 2.7 fusion.59
  705.6 4.7 reduce-scatter.24.cloned.1.call-done
  712.0 1.9 fusion.61
  713.9 8.4 fusion.41
  723.4 4.9 convolution_multiply_fusion
  728.5 8.4 fusion.63
  737.0 20.1 fusion.76
  757.0 549.5 %fusion = f32[48,2048]{1,0:T(8,128)S(1)} fusion(f32[5632,2048]{1,0:T(8,128)} %fusion.76), kind=kCustom, calls=%all-reduce-scatter | all-reduce-scatter fusion | flops 12582913 | bytes 46530560
  1307.2 2.0 collective-permute-start.10
  1311.9 3.5 collective-permute-start.7
  1315.3 4.9 collective-permute-start.6
  1320.2 5.8 collective-permute-start.5
  1326.1 12.2 fusion.15
  1338.3 3.8 collective-permute-start.4
  1342.1 44.0 %collective-permute-done.8 = f32[48,2048]{1,0:T(8,128)S(1)} collective-permute-done((f32[48,2048]{1,0:T(8,128)S(1)}, f32[48,2048]{1,0:T(8,128)S(1)}, u32[]{:S(2)}, u32[]{:S(2)}) %collective-permute-start.8) | collective-permute-done | bytes 393248
  1387.4 35.2 collective-permute-done.7
  1425.2 2.1 collective-permute-start
  1427.3 6.4 fusion.75
  1433.8 3.7 collective-permute-done.2
  1437.6 12.6 collective-permute-done.1
  1450.9 31.0 concatenate.31
  1482.0 1.8 constant_dynamic-slice_fusion
  1483.8 1.8 convolution_add_fusion.1
  1485.6 1.9 fusion.35
  1487.5 135.0 %all-reduce.6 = (f32[2048]{0:T(1024)S(1)}, f32[2048]{0:T(1024)S(1)}) all-reduce(f32[2048]{0:T(1024)S(1)} %get-tuple-element.13, f32[2048]{0:T(1024)S(1)} %copy-done.30), channel_id=4, replica_groups=mesh['dp'=16,'ctx'=8] {'dp','ctx'}, use_global_device_ids=true, to_apply=%region_14.15.clone | all-reduce | flops 4096 | bytes 32768
  1623.6 1.3 fusion.31
  1625.0 18.0 reduce-scatter.22.cloned.1.call-done
  1642.9 2.0 fusion.70
  1644.9 638.4 %reduce-scatter.18.cloned.1.call-done = f32[16,256]{1,0:T(8,128)} async-done(((f32[2048,256]{1,0:T(8,128)}), f32[16,256]{1,0:T(8,128)}) %reduce-scatter.18.cloned.1.call-update) | async-done | bytes 16400 | tf_op jit(solution)/shard_map/reduce_scatter | solution.py:245
  2283.3 636.5 %reduce-scatter.16.cloned.1.call-done = f32[16,256]{1,0:T(8,128)} async-done(((f32[2048,256]{1,0:T(8,128)}), f32[16,256]{1,0:T(8,128)}) %reduce-scatter.16.cloned.1.call-update) | async-done | bytes 16400 | tf_op jit(solution)/shard_map/reduce_scatter | solution.py:244
  2919.8 661.8 %reduce-scatter.20.cloned.1.call-done = f32[16,2048]{1,0:T(8,128)} async-done(((f32[2048,2048]{1,0:T(8,128)}), f32[16,2048]{1,0:T(8,128)}) %reduce-scatter.20.cloned.1.call-update) | async-done | bytes 131088 | tf_op jit(solution)/shard_map/reduce_scatter | solution.py:246
  3581.5 661.6 %reduce-scatter.14.cloned.1.call-done = f32[16,2048]{1,0:T(8,128)} async-done(((f32[2048,2048]{1,0:T(8,128)}), f32[16,2048]{1,0:T(8,128)}) %reduce-scatter.14.cloned.1.call-update) | async-done | bytes 131088 | tf_op jit(solution)/shard_map/reduce_scatter | solution.py:243
  (148 shorter events, 26.6 us)
Async XLA Ops:
  7.2 80.4 %all-gather.9.cloned.1.call-start = ((), (), s32[]{:S(2)}) async-start(), calls=%async_computation.7 | async-start | bytes 1056768 | tf_op jit(solution)/shard_map/all_gather | solution.py:95
  7.9 132.8 %all-gather.11.cloned.1.call-start = ((), (), s32[]{:S(2)}) async-start(), calls=%async_computation.8 | async-start | bytes 1056768 | tf_op jit(solution)/shard_map/all_gather | solution.py:94
  8.7 202.7 %all-gather.13.cloned.1.call-start = ((), (), s32[]{:S(2)}) async-start(), calls=%async_computation.9 | async-start | bytes 8454144 | tf_op jit(solution)/shard_map/all_gather | solution.py:93
  9.4 272.6 %all-gather.15.cloned.1.call-start = ((), (), s32[]{:S(2)}) async-start(), calls=%async_computation.10 | async-start | bytes 8454144 | tf_op jit(solution)/shard_map/all_gather | solution.py:139
  10.0 365.6 %all-gather.21.cloned.1.call-start = ((), (), s32[]{:S(2)}) async-start(), calls=%async_computation.18 | async-start | bytes 25362432 | tf_op jit(solution)/shard_map/all_gather | solution.py:148
  10.6 457.2 %all-gather.19.cloned.1.call-start = ((), (), s32[]{:S(2)}) async-start(), calls=%async_computation.12 | async-start | bytes 23248896 | tf_op jit(solution)/shard_map/all_gather | solution.py:147
  11.1 549.0 %all-gather.17.cloned.1.call-start = ((), (), s32[]{:S(2)}) async-start(), calls=%async_computation.11 | async-start | bytes 23248896 | tf_op jit(solution)/shard_map/all_gather | solution.py:146
  11.9 690.0 %reduce-scatter.26.cloned.1.call-start = ((), (), s32[]{:S(2)}) async-start(), calls=%async_computation.20 | async-start | bytes 589824 | tf_op jit(solution)/shard_map/convert_element_type | solution.py:225
  84.1 134.3 %copy-start.15 = (f32[2048]{0:T(1024)}, f32[2048]{0:T(1024)S(1)}, u32[]{:S(2)}) copy-start(f32[2048]{0:T(1024)S(1)} %convert_element_type.107) | copy-start | bytes 24580
  86.5 132.0 %copy-start.31 = (f32[128]{0:T(128)}, f32[128]{0:T(128)S(1)}, u32[]{:S(2)}) copy-start(f32[128]{0:T(128)S(1)} %add_rsqrt_fusion.1) | copy-start | bytes 1540
  87.2 131.4 %copy-start.17 = (f32[128,32]{0,1:T(8,128)}, f32[128,32]{0,1:T(8,128)S(1)}, u32[]{:S(2)}) copy-start(f32[128,32]{0,1:T(8,128)S(1)} %get-tuple-element.36) | copy-start | bytes 49156
  155.0 70.8 %copy-start.5 = (bf16[1024,4,64]{0,2,1:T(8,128)(2,1)}, bf16[1024,4,64]{0,2,1:T(8,128)(2,1)S(1)}, u32[]{:S(2)}) copy-start(bf16[1024,4,64]{0,2,1:T(8,128)(2,1)S(1)} %all_gather.46) | copy-start | bytes 1572868
  168.4 65.7 %copy-start.9 = (bf16[1024,4,64]{0,2,1:T(8,128)(2,1)}, bf16[1024,4,64]{0,2,1:T(8,128)(2,1)S(1)}, u32[]{:S(2)}) copy-start(bf16[1024,4,64]{0,2,1:T(8,128)(2,1)S(1)} %all_gather.44) | copy-start | bytes 1572868
  218.6 7.2 copy-start.11
  234.1 47.9 %copy-start.1 = (bf16[128,2048]{1,0:T(8,128)(2,1)S(1)}, bf16[128,2048]{1,0:T(8,128)(2,1)}, u32[]{:S(2)}) copy-start(bf16[128,2048]{1,0:T(8,128)(2,1)} %param.13) | copy-start | bytes 1572868
  241.6 45.1 %copy-start.7 = (bf16[4,64,8,128]{3,1,2,0:T(8,128)(2,1)}, bf16[4,64,8,128]{3,1,2,0:T(8,128)(2,1)S(1)}, u32[]{:S(2)}) copy-start(bf16[4,64,8,128]{3,1,2,0:T(8,128)(2,1)S(1)} %fusion.24) | copy-start | bytes 1572868
  587.5 13.4 copy-start.3
  587.5 13.4 copy-start.4
  600.9 14.1 copy-start.13
  624.9 9.3 copy-start.10
  647.1 63.2 %reduce-scatter.24.cloned.1.call-start = ((), (), s32[]{:S(2)}) async-start(), calls=%async_computation.19 | async-start | bytes 589824
  647.1 15.2 copy-start.12
  659.0 3.3 copy-start
  667.8 975.2 %reduce-scatter.22.cloned.1.call-start = ((), (), s32[]{:S(2)}) async-start(), calls=%async_computation.17 | async-start | bytes 92995584 | tf_op jit(solution)/shard_map/reduce_scatter | solution.py:180
  701.7 1.0 copy-start.2
  701.7 1.0 copy-start.16
  701.7 1.0 copy-start.32
  701.7 9.6 copy-start.18
  701.7 9.6 copy-start.29
  701.8 12.2 copy-start.8
  701.8 1581.5 %reduce-scatter.18.cloned.1.call-start = ((), (), s32[]{:S(2)}) async-start(), calls=%async_computation.15 | async-start | bytes 2113536 | tf_op jit(solution)/shard_map/reduce_scatter | solution.py:245
  705.5 2214.3 %reduce-scatter.16.cloned.1.call-start = ((), (), s32[]{:S(2)}) async-start(), calls=%async_computation.14 | async-start | bytes 2113536 | tf_op jit(solution)/shard_map/reduce_scatter | solution.py:244
  711.3 0.6 copy-start.14
  713.9 2867.7 %reduce-scatter.20.cloned.1.call-start = ((), (), s32[]{:S(2)}) async-start(), calls=%async_computation.16 | async-start | bytes 16908288 | tf_op jit(solution)/shard_map/reduce_scatter | solution.py:246
  722.4 1.0 copy-start.6
  722.4 3520.8 %reduce-scatter.14.cloned.1.call-start = ((), (), s32[]{:S(2)}) async-start(), calls=%async_computation.13 | async-start | bytes 16908288 | tf_op jit(solution)/shard_map/reduce_scatter | solution.py:243
  1307.2 13.0 collective-permute-start.10
  1309.2 29.0 collective-permute-start.9
  1310.5 75.5 %collective-permute-start.8 = (f32[48,2048]{1,0:T(8,128)S(1)}, f32[48,2048]{1,0:T(8,128)S(1)}, u32[]{:S(2)}, u32[]{:S(2)}) collective-permute-start(f32[48,2048]{1,0:T(8,128)S(1)} %fusion), channel_id=1, source_target_pairs={{0,9},{1,10},{2,11},{3,12},{4,13},{5,14},{6,15},{7,16},{8,17},{9,1... | collective-permute-start | bytes 1179656
  1311.9 110.7 %collective-permute-start.7 = (f32[48,2048]{1,0:T(8,128)S(1)}, f32[48,2048]{1,0:T(8,128)S(1)}, u32[]{:S(2)}, u32[]{:S(2)}) collective-permute-start(f32[48,2048]{1,0:T(8,128)S(1)} %fusion), channel_id=1, source_target_pairs={{0,8},{1,9},{2,10},{3,11},{4,12},{5,13},{6,14},{7,15},{8,16},{9,17... | collective-permute-start | bytes 1179656
  1315.3 108.5 %collective-permute-start.6 = (f32[48,2048]{1,0:T(8,128)S(1)}, f32[48,2048]{1,0:T(8,128)S(1)}, u32[]{:S(2)}, u32[]{:S(2)}) collective-permute-start(f32[48,2048]{1,0:T(8,128)S(1)} %fusion), channel_id=1, source_target_pairs={{0,7},{1,8},{2,9},{3,10},{4,11},{5,12},{6,13},{7,14},{8,15},{9,16}... | collective-permute-start | bytes 1179656
  1320.2 105.0 %collective-permute-start.5 = (f32[48,2048]{1,0:T(8,128)S(1)}, f32[48,2048]{1,0:T(8,128)S(1)}, u32[]{:S(2)}, u32[]{:S(2)}) collective-permute-start(f32[48,2048]{1,0:T(8,128)S(1)} %fusion), channel_id=1, source_target_pairs={{0,6},{1,7},{2,8},{3,9},{4,10},{5,11},{6,12},{7,13},{8,14},{9,15},... | collective-permute-start | bytes 1179656
  1338.2 111.9 %copy-start.19 = (f32[48,2048]{1,0:T(8,128)}, f32[48,2048]{1,0:T(8,128)S(1)}, u32[]{:S(2)}) copy-start(f32[48,2048]{1,0:T(8,128)S(1)} %collective-permute-done.9) | copy-start | bytes 1179652
  1338.3 95.5 %collective-permute-start.4 = (f32[48,2048]{1,0:T(8,128)S(1)}, f32[48,2048]{1,0:T(8,128)S(1)}, u32[]{:S(2)}, u32[]{:S(2)}) collective-permute-start(f32[48,2048]{1,0:T(8,128)S(1)} %fusion), channel_id=1, source_target_pairs={{0,5},{1,6},{2,7},{3,8},{4,9},{5,10},{6,11},{7,12},{8,13},{9,14},{... | collective-permute-start | bytes 1179656
  1386.1 64.1 %copy-start.20 = (f32[48,2048]{1,0:T(8,128)}, f32[48,2048]{1,0:T(8,128)S(1)}, u32[]{:S(2)}) copy-start(f32[48,2048]{1,0:T(8,128)S(1)} %collective-permute-done.8) | copy-start | bytes 1179652
  1386.1 47.7 %collective-permute-start.3 = (f32[48,2048]{1,0:T(8,128)S(1)}, f32[48,2048]{1,0:T(8,128)S(1)}, u32[]{:S(2)}, u32[]{:S(2)}) collective-permute-start(f32[48,2048]{1,0:T(8,128)S(1)} %fusion), channel_id=1, source_target_pairs={{0,4},{1,5},{2,6},{3,7},{4,8},{5,9},{6,10},{7,11},{8,12},{9,13},{1... | collective-permute-start | bytes 1179656
  1422.6 27.6 copy-start.21
  1422.6 15.0 collective-permute-start.2
  1423.9 26.2 copy-start.22
  1423.9 26.2 collective-permute-start.1
  1425.2 24.9 copy-start.23
  1425.2 25.7 collective-permute-start
  1433.7 51.8 %copy-start.28 = (bf16[128,256]{1,0:T(8,128)(2,1)S(1)}, bf16[128,256]{1,0:T(8,128)(2,1)}, u32[]{:S(2)}) copy-start(bf16[128,256]{1,0:T(8,128)(2,1)} %reduce-scatter.26.cloned.1.call-done) | copy-start | bytes 196612
  1433.8 53.7 %copy-start.30 = (f32[2048]{0:T(1024)S(1)}, f32[2048]{0:T(1024)}, u32[]{:S(2)}) copy-start(f32[2048]{0:T(1024)} %get-tuple-element.11) | copy-start | bytes 24580
  1433.8 16.4 copy-start.24
  1433.8 16.4 copy-start.25
  1437.6 12.6 copy-start.26
  1450.2 0.7 copy-start.27
Sparse Core Ops, SparseCore 0:
  10.8 66.0 all-gather.8
  79.6 61.0 all-gather.10
  143.7 67.6 all-gather.12
  214.2 67.6 all-gather.14
  284.9 90.6 all-gather.20
  378.4 89.3 all-gather.18
  470.7 89.3 all-gather.16
  647.2 30.2 reduce-scatter.25
  680.6 29.6 reduce-scatter.23
  712.5 930.3 reduce-scatter.21
  1645.9 637.3 reduce-scatter.17
  2286.2 633.5 reduce-scatter.15
  2922.7 658.7 reduce-scatter.19
  3584.3 658.7 reduce-scatter.13
where the time goes:
time: 4260 us; the launch traced here: 4250 us
  waiting for transfers between devices  3090 us (73%)
  blocking collectives  779 us (18%)
  matrix products  230 us (5%)
  local copies, waits for them, and re-layouts  83.3 us (2%)
    unnamed x3, blocking collectives  753 us
    reduce_scatter x1, waiting for transfers between devices, per_device(): lax.psum_scatter(out_term, ('dp', 'ctx'), scatter_dimension=0, tiled=True)  662 us
    reduce_scatter x1, waiting for transfers between devices, per_device(): lax.psum_scatter(query_term, ('dp', 'ctx'), scatter_dimension=0, tiled=True)  662 us
    reduce_scatter x1, waiting for transfers between devices, per_device(): lax.psum_scatter(value_term, ('dp', 'ctx'), scatter_dimension=0, tiled=True)  638 us
    reduce_scatter x1, waiting for transfers between devices, per_device(): lax.psum_scatter(key_term, ('dp', 'ctx'), scatter_dimension=0, tiled=True)  636 us
    dot_general x13, matrix products, contract(): lax.dot_general(left_op, right_op, dims_pair, preferred_element_type=jnp....  135 us
    unnamed x26, waiting for transfers between devices  105 us
    all_gather x1, waiting for transfers between devices, per_device(): lax.all_gather(w_down, ('dp', 'ctx'), axis=0, tiled=True)  88.7 us
  transfers between devices with their start and end apart: 25, of which 16 were waited for; matrix products, arithmetic and copies ran while one was open for 19% of the time, Pallas kernels for 0%

commit v1 on v0

v1 whole, which is shorter than its diff:
```python
import jax
import jax.numpy as jnp
from jax import lax
from jax.experimental import pallas as pl
from jax.experimental.pallas import tpu as pltpu
from jax.sharding import PartitionSpec as P

D = 2048
HEADS = 32
KV_HEADS = 4
HEAD_DIM = 64
FF = 5632
N_CTX = 8
N_DP = 16
ROWS = 128
GROUP = 1024
Q_LOC = 256
QKV_LOC = 384
FF_PART = 44
FF_PAD = 48
FF_LOC = N_DP * FF_PAD
EPSILON = 1e-05
NEG_LARGE = -1e30
MESH = pl.DeviceIdType.MESH
BF = jnp.bfloat16
F32 = jnp.float32
ANY = pl.BlockSpec(memory_space=pl.ANY)
VM = pl.BlockSpec(memory_space=pltpu.VMEM)
ACROSS = (((1,), (1,)), ((), ()))
DOWNWARD = (((0,), (0,)), ((), ()))


class Place:
    def __init__(self):
        self.d = lax.axis_index("dp")
        self.c = lax.axis_index("ctx")
        self.z, self.y = lax.div(self.d, 4), lax.rem(self.d, 4)
        self.x, self.k = lax.div(self.c, 2), lax.rem(self.c, 2)

    def at_x(self, step):
        return lax.rem(self.x + step, 4)

    def on_x(self, step):
        return (self.d, self.at_x(step) * 2 + self.k)

    def sibling(self):
        return (self.d, self.x * 2 + 1 - self.k)

    def on_ctx(self, step):
        return (self.d, lax.rem(self.c + step, 8))

    def on_y(self, step):
        return (self.z * 4 + lax.rem(self.y + step, 4), self.c)

    def on_z(self, step):
        return (lax.rem(self.z + step, 4) * 4 + self.y, self.c)

    def moved_to(self):
        flat = self.d * 8 + self.c
        return (lax.rem(flat, 16), lax.div(flat, 16))

    def moved_from(self):
        flat = self.c * 16 + self.d
        return (lax.div(flat, 8), lax.rem(flat, 8))

    def moves(self):
        return self.d * 8 + self.c != self.c * 16 + self.d


class Copies:
    def __init__(self, send_sems, recv_sems):
        self.send_sems, self.recv_sems, self.used, self.started = send_sems, recv_sems, 0, []

    def make(self, src, dst, device):
        i = self.used
        self.used += 1
        return pltpu.make_async_remote_copy(
            src_ref=src,
            dst_ref=dst,
            send_sem=self.send_sems.at[i],
            recv_sem=self.recv_sems.at[i],
            device_id=device,
            device_id_type=MESH,
        )

    def send(self, src, dst, device):
        copy = self.make(src, dst, device)
        copy.start()
        self.started.append(copy)
        return copy

    def finish(self):
        for copy in self.started:
            copy.wait_send()


def greet(peers, extra=None, extra_on=None):
    barrier = pltpu.get_barrier_semaphore()
    for peer in peers:
        pl.semaphore_signal(barrier, 1, device_id=peer, device_id_type=MESH)
    count = len(peers)
    if extra is not None:

        @pl.when(extra_on)
        def _():
            pl.semaphore_signal(barrier, 1, device_id=extra, device_id_type=MESH)

        count = jnp.where(extra_on, count + 1, count)
    pl.semaphore_wait(barrier, count)


def yz_peers(me):
    return [me.on_y(s) for s in (1, 2, 3)] + [me.on_z(s) for s in (1, 2, 3)]


def ctx_peers(me):
    return [me.on_ctx(s) for s in range(1, 8)]


def x_peers(me):
    return [me.on_x(1), me.on_x(3), me.sibling()]


def round_robin(*flows):
    flows = list(flows)
    while flows:
        flows = [f for f in flows if next(f, "end") != "end"]


def ctx_gather(me, copies, src, full, local_sem):
    own, left, right, far = (me.at_x(s) * 2 + me.k for s in (0, 3, 1, 2))
    to_right, to_left, to_sib = me.on_x(1), me.on_x(3), me.sibling()
    top, low = pl.ds(0, 64), pl.ds(64, 64)
    r1 = copies.send(src.at[top], full.at[own, top], to_right)
    l1 = copies.send(src.at[low], full.at[own, low], to_left)
    s0 = copies.send(src, full.at[own], to_sib)
    r2 = copies.send(src.at[low], full.at[own, low], to_right)
    l2 = copies.send(src.at[top], full.at[own, top], to_left)
    mine = pltpu.make_async_copy(src, full.at[own], local_sem)
    mine.start()
    yield
    r1.wait_recv()
    r3 = copies.send(full.at[left, top], full.at[left, top], to_right)
    l1.wait_recv()
    l3 = copies.send(full.at[right, low], full.at[right, low], to_left)
    yield
    r2.wait_recv()
    s1 = copies.send(full.at[left], full.at[left], to_sib)
    l2.wait_recv()
    s2 = copies.send(full.at[right], full.at[right], to_sib)
    yield
    r3.wait_recv()
    s3 = copies.send(full.at[far, top], full.at[far, top], to_sib)
    l3.wait_recv()
    s4 = copies.send(full.at[far, low], full.at[far, low], to_sib)
    yield
    for s in (s0, s1, s2, s3, s4):
        s.wait_recv()
    mine.wait()


def add_rows(dst, rows, *terms):
    def step(i, carry):
        at = pl.ds(pl.multiple_of(i * 16, 16), 16)
        total = terms[0](at).astype(F32)
        for term in terms[1:]:
            total += term(at).astype(F32)
        dst[at, :] = total.astype(dst.dtype)
        return carry

    lax.fori_loop(0, rows // 16, step, 0)


def ctx_scatter(me, copies, part, pair, half_left, half_right, from_left, from_right):
    to_right, to_left, to_sib = me.on_x(1), me.on_x(3), me.sibling()
    top, low = pl.ds(0, 64), pl.ds(64, 64)
    arriving = {}
    for s in (2, 1, 3, 0):
        arriving[s] = copies.send(part.at[me.at_x(s) * 2 + 1 - me.k], pair.at[s], to_sib)
    yield

    def merge(s):
        arriving[s].wait_recv()
        block = me.at_x(s) * 2 + me.k
        add_rows(pair.at[s], 128, lambda at: part[block, at, :], lambda at: pair[s, at, :])

    merge(2)
    a = copies.send(pair.at[2, top], half_left, to_right)
    b = copies.send(pair.at[2, low], half_right, to_left)
    merge(1)
    r1 = copies.send(pair.at[1, low], from_left.at[low], to_right)
    merge(3)
    l1 = copies.send(pair.at[3, top], from_right.at[top], to_left)
    merge(0)
    yield
    a.wait_recv()
    add_rows(half_left, 64, lambda at: half_left[at, :], lambda at: pair[1, at, :])
    r2 = copies.send(half_left, from_left.at[top], to_right)
    b.wait_recv()
    add_rows(
        half_right,
        64,
        lambda at: half_right[at, :],
        lambda at: pair.at[3, low][at, :],
    )
    l2 = copies.send(half_right, from_right.at[low], to_left)
    yield
    for copy in (r1, l1, r2, l2):
        copy.wait_recv()


SCATTER_SCRATCH = [
    pltpu.VMEM((4, 128, D), BF),
    pltpu.VMEM((64, D), BF),
    pltpu.VMEM((64, D), BF),
    pltpu.VMEM((128, D), BF),
    pltpu.VMEM((128, D), BF),
]


def scattered(at, pair, from_left, from_right):
    return (
        pair[0, at, :].astype(F32) + from_left[at, :].astype(F32) + from_right[at, :].astype(F32)
    )


def halves(ref, half, by_rows):
    shape = ref.shape
    if by_rows:
        n = shape[-3]
        return ref.at[(*(slice(None),) * (len(shape) - 3), pl.ds(half * (n // 2), n // 2))]
    columns = shape[-1]
    return ref.at[
        (*(slice(None),) * (len(shape) - 1), pl.ds(half * (columns // 2), columns // 2))
    ]


def dp_axes(me, half):
    z = (me.z, me.on_z)
    y = (me.y, me.on_y)
    return (y, z) if half else (z, y)


def dp_gather(me, copies, full, half, by_rows):
    view = halves(full, half, by_rows)
    (p2, dev2), (p1, dev1) = dp_axes(me, half)

    def group(i2, j1):
        return view.at[j1, i2] if half else view.at[i2, j1]

    own = group(p2, p1)
    first = [copies.send(own, own, dev1(s)) for s in (1, 3, 2)]
    yield
    for copy in first:
        copy.wait_recv()
    every, lo, hi = pl.ds(0, 4), pl.ds(0, 2), pl.ds(2, 2)
    mine = group(p2, every)
    up = copies.send(mine, mine, dev2(1))
    down = copies.send(mine, mine, dev2(3))
    yield
    up.wait_recv()
    passed = group(lax.rem(p2 + 3, 4), lo)
    up2 = copies.send(passed, passed, dev2(1))
    down.wait_recv()
    passed = group(lax.rem(p2 + 1, 4), hi)
    down2 = copies.send(passed, passed, dev2(3))
    yield
    up2.wait_recv()
    down2.wait_recv()


def add_blocks(dst, *terms):
    lead = dst.shape[:-2]
    if not lead:
        total = terms[0][...].astype(F32)
        for term in terms[1:]:
            total += term[...].astype(F32)
        dst[...] = total.astype(dst.dtype)
        return

    def step(i, carry):
        at = (lax.div(i, lead[1]), lax.rem(i, lead[1])) if len(lead) == 2 else (i,)
        total = terms[0][at].astype(F32)
        for term in terms[1:]:
            total += term[at].astype(F32)
        dst[at] = total.astype(dst.dtype)
        return carry

    lax.fori_loop(0, lead[0] * (lead[1] if len(lead) == 2 else 1), step, 0)


def dp_scatter(me, copies, part, half, by_rows, out, pass_up, pass_down, from_up, from_down, last):
    view = halves(part, half, by_rows)
    (p1, dev1), (p2, dev2) = dp_axes(me, half)

    def group(i1, j2):
        return view.at[j2, i1] if half else view.at[i1, j2]

    every, lo, hi = pl.ds(0, 4), pl.ds(0, 2), pl.ds(2, 2)
    nxt, far, prv = (lax.rem(p1 + s, 4) for s in (1, 2, 3))
    a = copies.send(group(far, lo), pass_up, dev1(1))
    b = copies.send(group(far, hi), pass_down, dev1(3))
    e1 = copies.send(group(nxt, hi), from_up.at[hi], dev1(1))
    e2 = copies.send(group(prv, lo), from_down.at[lo], dev1(3))
    yield
    a.wait_recv()
    add_blocks(pass_up, pass_up, group(nxt, lo))
    f1 = copies.send(pass_up, from_up.at[lo], dev1(1))
    b.wait_recv()
    add_blocks(pass_down, pass_down, group(prv, hi))
    f2 = copies.send(pass_down, from_down.at[hi], dev1(3))
    yield
    for copy in (e1, e2, f1, f2):
        copy.wait_recv()
    add_blocks(from_up, from_up, from_down, group(p1, every))
    sent = [
        copies.send(from_up.at[lax.rem(p2 + s, 4)], last.at[s - 1], dev2(s)) for s in (1, 2, 3)
    ]
    yield
    for copy in sent:
        copy.wait_recv()
    add_blocks(halves(out, half, by_rows), from_up.at[p2], last.at[0], last.at[1], last.at[2])


def dp_scatter_scratch(block, by_rows):
    block = (block[0] // 2, *block[1:]) if by_rows else (*block[:-1], block[-1] // 2)
    return [pltpu.VMEM((lead, *block), BF) for lead in (2, 2, 4, 4, 3)] * 2


def start_kernel(
    qkv_src, gu_src, out_src, dn_src, n1, n1_full, w_qkv, w_out, gu_own, dn_own, ss, rs, ls
):
    me = Place()
    greet(ctx_peers(me) + yz_peers(me), me.moved_from(), me.moves())
    copies = Copies(ss, rs)
    home = w_qkv.at[me.z, me.y]
    qkv_in = [
        copies.send(qkv_src.at[lax.rem(me.c + s, 8)], home.at[me.c], me.on_ctx(s))
        for s in range(1, 8)
    ]
    qkv_mine = pltpu.make_async_copy(qkv_src.at[me.c], home.at[me.c], ls.at[0])
    qkv_mine.start()
    out_home = w_out.at[me.z, me.y]
    there = me.moved_to()
    move_out = copies.make(out_src, w_out.at[lax.div(there[0], 4), lax.rem(there[0], 4)], there)
    move_dn = copies.make(dn_src, dn_own, there)
    keep_out = pltpu.make_async_copy(out_src, out_home, ls.at[1])
    keep_dn = pltpu.make_async_copy(dn_src, dn_own, ls.at[2])

    @pl.when(me.moves())
    def _():
        move_out.start()
        move_dn.start()

    @pl.when(jnp.logical_not(me.moves()))
    def _():
        keep_out.start()
        keep_dn.start()

    rows = ctx_gather(me, copies, n1, n1_full, ls.at[3])
    next(rows)
    gu_in = [
        copies.send(gu_src.at[lax.rem(me.c + s, 8)], gu_own.at[me.c], me.on_ctx(s))
        for s in range(1, 8)
    ]
    gu_mine = pltpu.make_async_copy(gu_src.at[me.c], gu_own.at[me.c], ls.at[4])
    gu_mine.start()
    for copy in qkv_in:
        copy.wait_recv()
    qkv_mine.wait()
    flows = [dp_gather(me, copies, w_qkv, h, True) for h in (0, 1)]
    for flow in flows:
        next(flow)

    @pl.when(me.moves())
    def _():
        move_out.wait()
        move_dn.wait()

    @pl.when(jnp.logical_not(me.moves()))
    def _():
        keep_out.wait()
        keep_dn.wait()

    flows += [dp_gather(me, copies, w_out, h, False) for h in (0, 1)]
    round_robin(*flows, rows)
    for copy in gu_in:
        copy.wait_recv()
    gu_mine.wait()
    copies.finish()


def middle_kernel(
    part, tokens, cot, gu_own, dn_own, h1, n2_full, cot_full, w_gu, w_dn,
    n2, pair, half_left, half_right, from_left, from_right, ss, rs, ls,
):
    me = Place()
    greet(x_peers(me) + yz_peers(me))
    copies = Copies(ss, rs)
    keep_gu = pltpu.make_async_copy(gu_own, w_gu.at[me.z, me.y], ls.at[0])
    keep_dn = pltpu.make_async_copy(dn_own, w_dn.at[me.z, me.y], ls.at[1])
    keep_gu.start()
    keep_dn.start()
    rows = ctx_scatter(me, copies, part, pair, half_left, half_right, from_left, from_right)
    next(rows)
    keep_gu.wait()
    keep_dn.wait()
    flows = [dp_gather(me, copies, w_gu, h, True) for h in (0, 1)]
    for flow in flows:
        next(flow)
    next(rows)
    flows += [dp_gather(me, copies, w_dn, h, False) for h in (0, 1)]
    for flow in flows[2:]:
        next(flow)
    seeds = ctx_gather(me, copies, cot, cot_full, ls.at[2])
    next(seeds)
    next(rows)
    for flow in flows:
        next(flow)
    for _ in rows:
        pass

    def norm(i, carry):
        at = pl.ds(pl.multiple_of(i * 16, 16), 16)
        hidden = tokens[at, :].astype(F32) + scattered(at, pair, from_left, from_right)
        scale = lax.rsqrt(jnp.mean(hidden * hidden, -1, keepdims=True) + EPSILON)
        h1[at, :] = hidden
        n2[at, :] = (hidden * scale).astype(BF)
        return carry

    lax.fori_loop(0, 8, norm, 0)
    normed = ctx_gather(me, copies, n2, n2_full, ls.at[3])
    next(normed)
    round_robin(seeds, normed, *flows)
    copies.finish()


def back_kernel(
    part_u, part_y, h1, cot, g_gu, g_dn, out, dh1, da_full, ret_gu, ret_dn,
    da, own_gu, own_dn, *rest,
):
    ss, rs, ls = rest[-3:]
    scr_u, scr_y = rest[0:5], rest[5:10]
    scr_gu, scr_dn = rest[10:20], rest[20:30]
    me = Place()
    greet(ctx_peers(me) + yz_peers(me), me.moved_to(), me.moves())
    copies = Copies(ss, rs)
    rows_u = ctx_scatter(me, copies, part_u, *scr_u)
    next(rows_u)
    flows = [
        dp_scatter(me, copies, g_gu, h, True, own_gu, *scr_gu[h * 5 : h * 5 + 5]) for h in (0, 1)
    ]
    for flow in flows:
        next(flow)
    next(rows_u)
    flows_dn = [
        dp_scatter(me, copies, g_dn, h, False, own_dn, *scr_dn[h * 5 : h * 5 + 5]) for h in (0, 1)
    ]
    for flow in flows_dn:
        next(flow)
    next(rows_u)
    rows_y = ctx_scatter(me, copies, part_y, *scr_y)
    next(rows_y)
    for flow in flows:
        next(flow)
    for _ in rows_u:
        pass

    def norm_back(i, carry):
        at = pl.ds(pl.multiple_of(i * 16, 16), 16)
        hidden = h1[at, :]
        scale = lax.rsqrt(jnp.mean(hidden * hidden, -1, keepdims=True) + EPSILON)
        u = scattered(at, scr_u[0], scr_u[3], scr_u[4])
        grad = (
            cot[at, :].astype(F32)
            + scale * u
            - hidden * (scale * scale * scale * jnp.mean(u * hidden, -1, keepdims=True))
        )
        dh1[at, :] = grad
        da[at, :] = grad.astype(BF)
        return carry

    lax.fori_loop(0, 8, norm_back, 0)
    rows_da = ctx_gather(me, copies, da, da_full, ls.at[0])
    next(rows_da)
    round_robin(rows_y, rows_da, *flows, *flows_dn)
    gu_in = [
        copies.send(own_gu.at[lax.rem(me.c + s, 8)], ret_gu.at[me.c], me.on_ctx(s))
        for s in range(1, 8)
    ]
    gu_mine = pltpu.make_async_copy(own_gu.at[me.c], ret_gu.at[me.c], ls.at[1])
    gu_mine.start()
    move_dn = copies.make(own_dn, ret_dn, me.moved_from())
    keep_dn = pltpu.make_async_copy(own_dn, ret_dn, ls.at[2])

    @pl.when(me.moves())
    def _():
        move_dn.start()

    @pl.when(jnp.logical_not(me.moves()))
    def _():
        keep_dn.start()

    def finish(i, carry):
        at = pl.ds(pl.multiple_of(i * 16, 16), 16)
        out[at, :] = (h1[at, :] + scattered(at, scr_y[0], scr_y[3], scr_y[4])).astype(BF)
        return carry

    lax.fori_loop(0, 8, finish, 0)
    for copy in gu_in:
        copy.wait_recv()
    gu_mine.wait()

    @pl.when(me.moves())
    def _():
        move_dn.wait()

    @pl.when(jnp.logical_not(me.moves()))
    def _():
        keep_dn.wait()

    copies.finish()


def end_kernel(
    part, tokens, dh1, g_qkv, g_out, grad, ret_qkv, ret_out, own_qkv, own_out, *rest
):
    ss, rs, ls = rest[-3:]
    scr, scr_qkv, scr_out = rest[0:5], rest[5:15], rest[15:25]
    me = Place()
    greet(ctx_peers(me) + yz_peers(me), me.moved_to(), me.moves())
    copies = Copies(ss, rs)
    rows = ctx_scatter(me, copies, part, *scr)
    next(rows)
    flows = [
        dp_scatter(me, copies, g_qkv, h, True, own_qkv, *scr_qkv[h * 5 : h * 5 + 5]) for h in (0, 1)
    ] + [
        dp_scatter(me, copies, g_out, h, False, own_out, *scr_out[h * 5 : h * 5 + 5])
        for h in (0, 1)
    ]
    round_robin(rows, *flows)
    qkv_in = [
        copies.send(own_qkv.at[lax.rem(me.c + s, 8)], ret_qkv.at[me.c], me.on_ctx(s))
        for s in range(1, 8)
    ]
    qkv_mine = pltpu.make_async_copy(own_qkv.at[me.c], ret_qkv.at[me.c], ls.at[0])
    qkv_mine.start()
    move_out = copies.make(own_out, ret_out, me.moved_from())
    keep_out = pltpu.make_async_copy(own_out, ret_out, ls.at[1])

    @pl.when(me.moves())
    def _():
        move_out.start()

    @pl.when(jnp.logical_not(me.moves()))
    def _():
        keep_out.start()

    def finish(i, carry):
        at = pl.ds(pl.multiple_of(i * 16, 16), 16)
        x = tokens[at, :].astype(F32)
        scale = lax.rsqrt(jnp.mean(x * x, -1, keepdims=True) + EPSILON)
        u = scattered(at, scr[0], scr[3], scr[4])
        grad[at, :] = (
            dh1[at, :]
            + scale * u
            - x * (scale * scale * scale * jnp.mean(u * x, -1, keepdims=True))
        )
        return carry

    lax.fori_loop(0, 8, finish, 0)
    for copy in qkv_in:
        copy.wait_recv()
    qkv_mine.wait()

    @pl.when(me.moves())
    def _():
        move_out.wait()

    @pl.when(jnp.logical_not(me.moves()))
    def _():
        keep_out.wait()

    copies.finish()


def call(kernel, number, ins, in_specs, outs, out_specs, scratch, n_copies, n_local):
    return pl.pallas_call(
        kernel,
        out_shape=[jax.ShapeDtypeStruct(*o) for o in outs],
        in_specs=in_specs,
        out_specs=out_specs,
        scratch_shapes=[
            *scratch,
            pltpu.SemaphoreType.DMA((n_copies,)),
            pltpu.SemaphoreType.DMA((n_copies,)),
            pltpu.SemaphoreType.DMA((n_local,)),
        ],
        compiler_params=pltpu.CompilerParams(
            collective_id=number, has_side_effects=True, vmem_limit_bytes=56 << 20
        ),
        name=kernel.__name__,
    )(*ins)


def rope_tables(position):
    inverse = jnp.power(F32(10000.0), -jnp.arange(0, HEAD_DIM, 2).astype(F32) / HEAD_DIM)
    angles = position.astype(F32)[:, None] * inverse[None, :]
    return (jnp.cos(angles)[:, None, :], jnp.sin(angles)[:, None, :])


def rotate(values, cos_table, sin_table):
    half_dim = values.shape[-1] // 2
    leading = values[..., :half_dim]
    trailing = values[..., half_dim:]
    return jnp.concatenate(
        [leading * cos_table - trailing * sin_table, trailing * cos_table + leading * sin_table], -1
    )


def contract(left_op, right_op, dims_pair):
    return lax.dot_general(left_op, right_op, dims_pair, preferred_element_type=F32)


def spread():
    place = jnp.arange(FF // N_CTX, dtype=jnp.int32)
    place = FF_PAD * (place // FF_PART) + place % FF_PART
    return place[:, None] == jnp.arange(FF_LOC, dtype=jnp.int32)[None, :]


def per_device(
    tokens, cotangent, lengths, spans, gain_attn, w_query, w_key, w_value, w_out, gain_mlp,
    w_gate, w_up, w_down,
):
    row_ids = jnp.arange(GROUP, dtype=jnp.int32)
    slot_ids = jnp.arange(2 * N_CTX, dtype=jnp.int32)
    table = spans.reshape(-1)
    span_ids = jnp.sum(
        jnp.where((row_ids // 64)[:, None] == slot_ids[None, :], table[None, :], 0), 1
    )
    packed = span_ids * 64 + row_ids % 64
    length_row = lengths[0]
    seq_ends = jnp.cumsum(length_row)
    before = seq_ends[None, :] <= packed[:, None]
    doc_ids = jnp.sum(before.astype(jnp.int32), 1)
    position = packed - jnp.sum(jnp.where(before, length_row[None, :], 0), 1)
    allowed = (doc_ids[:, None] == doc_ids[None, :]) & (packed[None, :] <= packed[:, None])
    cos_table, sin_table = rope_tables(position)

    gain_a = gain_attn.astype(F32)[:, None]
    gain_m = gain_mlp.astype(F32)[:, None]
    hot = spread()

    def scaled(w, gain):
        return (w.astype(F32) * gain).astype(BF)

    by_index = lambda w, n: w.reshape(16, n, -1).transpose(1, 0, 2)
    twice = lambda w: jnp.repeat(by_index(w, 4), 2, axis=0)
    qkv_src = jnp.concatenate(
        [
            by_index(scaled(w_query, gain_a), 8),
            twice(scaled(w_key, gain_a)),
            twice(scaled(w_value, gain_a)),
        ],
        -1,
    )

    def padded(w):
        cut = by_index(scaled(w, gain_m), 8)
        return contract(cut.reshape(128, -1), hot.astype(BF), (((1,), (0,)), ((), ()))).astype(
            BF
        ).reshape(8, 16, FF_LOC)

    gu_src = jnp.concatenate([padded(w_gate), padded(w_up)], -1)
    dn_src = jnp.pad(w_down, ((0, FF_PAD - FF_PART), (0, 0))).reshape(3, 16, D)
    tokens_f = tokens.astype(F32)
    scale_attn = lax.rsqrt(jnp.mean(tokens_f * tokens_f, -1, keepdims=True) + EPSILON)
    n1_own = (tokens_f * scale_attn).astype(BF)

    n1, wf_qkv, wf_out, gu_own, dn_own = call(
        start_kernel, 1,
        (qkv_src, gu_src, w_out, dn_src, n1_own), [ANY] * 5,
        [((8, 128, D), BF), ((4, 4, 8, 16, QKV_LOC), BF), ((4, 4, 16, D), BF),
         ((8, 16, 2 * FF_LOC), BF), ((3, 16, D), BF)],
        [ANY] * 5, [], 64, 5,
    )
    n1 = n1.reshape(GROUP, D)
    wf_qkv = wf_qkv.reshape(D, QKV_LOC)
    wf_out = wf_out.reshape(Q_LOC, D)

    heads = HEADS // N_CTX
    score_scale = HEAD_DIM ** (-0.5)
    qkv = jnp.dot(n1, wf_qkv, preferred_element_type=F32)
    q = rotate(qkv[:, :Q_LOC].reshape(GROUP, heads, HEAD_DIM), cos_table, sin_table).astype(BF)
    k = rotate(qkv[:, Q_LOC : Q_LOC + 64].reshape(GROUP, 1, HEAD_DIM), cos_table, sin_table)
    k = k.astype(BF)[:, 0]
    v = qkv[:, Q_LOC + 64 :].astype(BF)

    def scores_of():
        raw = jnp.einsum("qgd,nd->gqn", q, k, preferred_element_type=F32) * score_scale
        return jnp.where(allowed[None], raw, NEG_LARGE)

    scores = scores_of()
    peak = jnp.max(scores, -1, keepdims=True)
    expo = jnp.exp(scores - peak)
    denom = jnp.sum(expo, -1, keepdims=True)
    log_total = peak + jnp.log(denom)
    probs_low = (expo / denom).astype(BF)
    o = jnp.einsum("gqn,nd->qgd", probs_low, v, preferred_element_type=F32)
    o = o.astype(BF).reshape(GROUP, Q_LOC)
    branch_part = jnp.dot(o, wf_out, preferred_element_type=F32).astype(BF)

    h1, n2, cot_full, wf_gu, wf_dn = call(
        middle_kernel, 2,
        (branch_part.reshape(8, 128, D), tokens, cotangent, gu_own, dn_own),
        [VM, VM, ANY, ANY, ANY],
        [((128, D), F32), ((8, 128, D), BF), ((8, 128, D), BF),
         ((4, 4, 8, 16, 2 * FF_LOC), BF), ((4, 4, 3, 16, D), BF)],
        [VM, ANY, ANY, ANY, ANY],
        [pltpu.VMEM((128, D), BF), *SCATTER_SCRATCH], 64, 4,
    )
    n2 = n2.reshape(GROUP, D)
    cot_full = cot_full.reshape(GROUP, D)
    wf_gu = wf_gu.reshape(D, 2 * FF_LOC)
    wf_dn = wf_dn.reshape(FF_LOC, D)

    gu = jnp.dot(n2, wf_gu, preferred_element_type=F32)
    gate_act, up_act = gu[:, :FF_LOC], gu[:, FF_LOC:]
    gate_sig = jax.nn.sigmoid(gate_act)
    silu_act = gate_act * gate_sig
    hm = (silu_act * up_act).astype(BF)
    y_part = jnp.dot(hm, wf_dn, preferred_element_type=F32).astype(BF)
    inner_grad = contract(cot_full, wf_dn, ACROSS)
    gate_grad = inner_grad * up_act * gate_sig * (1.0 + gate_act * (1.0 - gate_sig))
    both_grads = jnp.concatenate([gate_grad, inner_grad * silu_act], 1).astype(BF)
    u_part = contract(both_grads, wf_gu, ACROSS).astype(BF)
    g_gu = contract(n2, both_grads, DOWNWARD).astype(BF)
    g_dn = contract(hm, cot_full, DOWNWARD).astype(BF)

    block_out, dh1, da, ret_gu, ret_dn = call(
        back_kernel, 3,
        (u_part.reshape(8, 128, D), y_part.reshape(8, 128, D), h1, cotangent,
         g_gu.reshape(4, 4, 8, 16, 2 * FF_LOC), g_dn.reshape(4, 4, 3, 16, D)),
        [VM] * 6,
        [((128, D), BF), ((128, D), F32), ((8, 128, D), BF),
         ((8, 16, 2 * FF_LOC), BF), ((3, 16, D), BF)],
        [VM, VM, ANY, ANY, ANY],
        [pltpu.VMEM((128, D), BF), pltpu.VMEM((8, 16, 2 * FF_LOC), BF), pltpu.VMEM((3, 16, D), BF),
         *SCATTER_SCRATCH, *SCATTER_SCRATCH,
         *dp_scatter_scratch((8, 16, 2 * FF_LOC), True), *dp_scatter_scratch((3, 16, D), False)],
        96, 3,
    )
    da = da.reshape(GROUP, D)

    do = contract(da, wf_out, ACROSS).astype(BF).reshape(GROUP, heads, HEAD_DIM)
    g_out = contract(o, da, DOWNWARD).astype(BF)
    probs = jnp.exp(scores_of() - log_total)
    probs_low = probs.astype(BF)
    prob_grad = jnp.einsum("qgd,nd->gqn", do, v, preferred_element_type=F32)
    delta = jnp.sum(probs * prob_grad, -1, keepdims=True)
    score_grad = (probs * (prob_grad - delta)).astype(BF)
    dq = jnp.einsum("gqn,nd->qgd", score_grad, k, preferred_element_type=F32) * score_scale
    dk = jnp.einsum("gqn,qgd->nd", score_grad, q, preferred_element_type=F32) * score_scale
    dv = jnp.einsum("gqn,qgd->nd", probs_low, do, preferred_element_type=F32)
    dq = rotate(dq, cos_table, -sin_table).reshape(GROUP, Q_LOC)
    dk = rotate(dk[:, None], cos_table, -sin_table)[:, 0]
    dqkv = jnp.concatenate([dq, dk, dv], 1).astype(BF)
    u1_part = contract(dqkv, wf_qkv, ACROSS).astype(BF)
    g_qkv = contract(n1, dqkv, DOWNWARD).astype(BF)

    input_grad, ret_qkv, ret_out = call(
        end_kernel, 4,
        (u1_part.reshape(8, 128, D), tokens, dh1,
         g_qkv.reshape(4, 4, 8, 16, QKV_LOC), g_out.reshape(4, 4, 16, D)),
        [VM] * 5,
        [((128, D), F32), ((8, 16, QKV_LOC), BF), ((16, D), BF)],
        [VM, ANY, ANY],
        [pltpu.VMEM((8, 16, QKV_LOC), BF), pltpu.VMEM((16, D), BF),
         *SCATTER_SCRATCH,
         *dp_scatter_scratch((8, 16, QKV_LOC), True), *dp_scatter_scratch((16, D), False)],
        64, 2,
    )

    ret_gu = ret_gu.astype(F32)
    ret_qkv = ret_qkv.astype(F32)
    back = lambda r: r.transpose(1, 0, 2).reshape(16, -1)
    raw_q = back(ret_qkv[:, :, :Q_LOC])
    pairs = ret_qkv[:, :, Q_LOC:].reshape(4, 2, 16, 128).sum(1)
    raw_k, raw_v = back(pairs[:, :, :64]), back(pairs[:, :, 64:])

    def unpadded(r):
        cut = lax.dot_general(
            r.reshape(128, FF_LOC).astype(BF),
            hot.astype(BF),
            ACROSS,
            preferred_element_type=F32,
        )
        return back(cut.reshape(8, 16, FF // N_CTX))

    raw_gate, raw_up = unpadded(ret_gu[:, :, :FF_LOC]), unpadded(ret_gu[:, :, FF_LOC:])

    def gain_grad(*pairs_of):
        return sum(jnp.sum(w.astype(F32) * raw, 1) for w, raw in pairs_of)

    return (
        block_out,
        input_grad,
        gain_grad((w_query, raw_q), (w_key, raw_k), (w_value, raw_v)),
        gain_a * raw_q,
        gain_a * raw_k,
        gain_a * raw_v,
        ret_out.astype(F32),
        gain_grad((w_gate, raw_gate), (w_up, raw_up)),
        gain_m * raw_gate,
        gain_m * raw_up,
        ret_dn.reshape(FF_PAD, D)[:FF_PART].astype(F32),
    )


def solution(mesh):
    flat = P(("dp", "ctx"), None)
    in_specs = (
        flat, flat, P("dp", None), P("dp", None, None), P(("dp", "ctx")), flat, flat, flat, flat,
        P(("dp", "ctx")), flat, flat, flat,
    )
    out_specs = (
        flat, flat, P(("dp", "ctx")), flat, flat, flat, flat, P(("dp", "ctx")), flat, flat, flat,
    )
    return jax.shard_map(
        per_device, mesh=mesh, in_specs=in_specs, out_specs=out_specs, check_vma=False
    )
```

time: 4260 us -> 430 us (0.10)
  waiting for transfers between devices: 3090 us -> 0 us
  blocking collectives: 779 us -> 0 us
  Pallas kernels: 0 us -> 262 us
  matrix products: 230 us -> 113 us
  local copies, waits for them, and re-layouts: 83.3 us -> 8.96 us
    reduce_scatter x5 -> x0, waiting for transfers between devices: 2620 us -> none  [the longest x1 662 us: per_device(): lax.psum_scatter(out_term, ('dp', 'ctx'), scatter_dimension=0, tiled=True)]
    unnamed x3 -> x0, blocking collectives: 753 us -> none
    all_gather x7 -> x0, waiting for transfers between devices: 365 us -> none  [the longest x1 88.7 us: per_device(): lax.all_gather(w_down, ('dp', 'ctx'), axis=0, tiled=True)]
    pallas_call x0 -> x4, Pallas kernels: none -> 262 us  [call(): pl.pallas_call(kernel, out_shape=[jax.ShapeDtypeStruct(*o) for o in outs]...]
    dot_general x26 -> x22, matrix products: 230 us -> 113 us  [the longest x10 43.9 us: contract(): lax.dot_general(left_op, right_op, dims_pair, preferred_element_type=F32)]
    unnamed x26 -> x0, waiting for transfers between devices: 105 us -> none
    unnamed x80 -> x74, local copies, waits for them, and re-layouts: 79.6 us -> 4.48 us
  transfers between devices with their start and end apart: 25 -> 0, of which waited for: 16 -> 0; matrix products, arithmetic and copies ran while one was open for 19% -> 0% of each run, Pallas kernels for 0% -> 0%
where the time goes in v1:
time: 430 us; the launch traced here: 422 us
  Pallas kernels  262 us (61%)
  matrix products  113 us (26%)
  other arithmetic  37.4 us (9%)
  local copies, waits for them, and re-layouts  8.96 us (2%)
    pallas_call x4, Pallas kernels, call(): pl.pallas_call(kernel, out_shape=[jax.ShapeDtypeStruct(*o) for o in outs]...  262 us
    dot_general x10, matrix products, contract(): lax.dot_general(left_op, right_op, dims_pair, preferred_element_type=F32)  43.9 us
    dot_general x1, matrix products, per_device(): prob_grad = jnp.einsum('qgd,nd->gqn', do, v, preferred_element_type=F32)  14.8 us
    dot_general x1, matrix products, per_device(): gu = jnp.dot(n2, wf_gu, preferred_element_type=F32)  10.3 us
    dot_general x1, matrix products, per_device(): dv = jnp.einsum('gqn,qgd->nd', probs_low, do, preferred_element_type=F32)  9.16 us

profile of v1, /device:TPU:0, one launch (start us, length us, event | category | flops | bytes accessed | tf_op | source)
XLA Modules:
  0.0 422.4 jit_solution(14305831561423662756)
XLA Ops:
  0.7 0.7 convert_element_type.146
  1.4 0.7 convert_element_type.153
  2.0 0.8 reduce-window.8
  2.9 1.2 fusion.39
  4.1 0.8 copy.85
  5.1 0.8 fusion.74
  5.8 0.8 fusion.75
  6.8 0.9 fusion.56
  7.8 0.7 pad_maximum_fusion.11.qkv_src
  8.5 1.6 pad.4
  10.1 1.1 fusion.41
  11.3 0.2 reshape.481
  11.5 0.6 fusion.25
  12.1 0.2 reshape.484
  12.4 0.6 fusion.26
  13.0 0.8 pad_maximum_fusion.6.gu_src
  13.8 1.2 fusion.69
  15.0 0.9 fusion.40.n1
  15.9 1.2 compare_and_fusion
  17.1 44.7 %start_kernel.1 = (bf16[8,128,2048]{2,1,0:T(8,128)(2,1)}, bf16[4,4,8,16,384]{4,3,2,1,0:T(8,128)(2,1)}, bf16[4,4,16,2048]{3,2,1,0:T(8,128)(2,1)}, bf16[8,16,1536]{2,1,0:T(8,128)(2,1)}, bf16[3,16,2048]{2,1,0:T(8,128)(2,1)}) custom-call(bf16[8,16,384]{2,1,0:T(8,128)(2,1)} %pad_maximum_fusion.11.qkv_src, bf16[8,16,1536]{2,1,0:T(8,128)(2,1)} %pad_maximum_fusion.6.gu_src, ...), custom_call_target="tpu_custom_call" | custom-call | tf_op jit(solution)/shard_map/start_kernel/pallas_call | solution.py:588
  61.8 4.5 %fusion.104 = f32[1024,384]{0,1:T(8,128)S(1)} fusion(bf16[1024,2048]{1,0:T(8,128)(2,1)} %bitcast.178, bf16[2048,384]{1,0:T(8,128)(2,1)} %bitcast.188), kind=kOutput, calls=%fused_computation.172 | convolution fusion | flops 1610612736 | bytes 7340032 | tf_op jit(solution)/shard_map/dot_general | solution.py:693
  66.3 0.6 fusion.68
  67.0 0.1 subtract_convert_fusion.1
  67.1 7.8 %fusion.103 = (f32[4,1024]{1,0:T(4,128)S(1)}, f32[4,1024,1024]{1,2,0:T(8,128)}) fusion(bf16[1024,4,32]{0,2,1:T(8,128)(2,1)S(1)} %get-tuple-element.55, bf16[1024,4,32]{0,2,1:T(8,128)(2,1)S(1)} %get-tuple-element.54, bf16[1024,32]{0,1:T(8,128)(2,1)S(1)} %get-tuple-element.63, bf16[1024,32]{0,1:T(8,128)(2,1)S(1)} %get-tuple-element.62, ...), kind=kOutput, calls=%fused_computation.171 | convolution fusion | flops 550760448 | bytes 18497536 | tf_op jit(solution)/shard_map/qgd,nd->gqn/dot_general | solution.py:700
  75.0 8.0 %fusion.3 = f32[4,1024]{1,0:T(4,128)S(1)} fusion(f32[4,1024,1024]{1,2,0:T(8,128)} %get-tuple-element.84, f32[4,1024]{1,0:T(4,128)S(1)} %get-tuple-element.83), kind=kLoop, calls=%fused_computation.9 | loop fusion | flops 8384512 | bytes 16809984 | tf_op jit(solution)/shard_map/reduce_sum | solution.py:706
  83.0 7.5 %fusion.18 = bf16[64,4,1024]{2,0,1:T(8,128)(2,1)S(1)} fusion(f32[4,1024,1024]{1,2,0:T(8,128)} %get-tuple-element.84, f32[4,1024]{1,0:T(4,128)S(1)} %fusion.3, f32[4,1024]{1,0:T(4,128)S(1)} %get-tuple-element.83, f32[1024,384]{0,1:T(8,128)S(1)} %fusion.104), kind=kOutput, calls=%fused_computation.40 | convolution fusion | flops 549715968 | bytes 17465344 | tf_op jit(solution)/shard_map/gqn,nd->qgd/dot_general | solution.py:709
  90.5 3.3 convolution_convert_fusion.3
  93.8 84.8 %middle_kernel.1 = (f32[128,2048]{1,0:T(8,128)}, bf16[8,128,2048]{2,1,0:T(8,128)(2,1)}, bf16[8,128,2048]{2,1,0:T(8,128)(2,1)}, bf16[4,4,8,16,1536]{4,3,2,1,0:T(8,128)(2,1)}, bf16[4,4,3,16,2048]{4,3,2,1,0:T(8,128)(2,1)}) custom-call(bf16[8,128,2048]{2,1,0:T(8,128)(2,1)} %bitcast.141, bf16[128,2048]{1,0:T(8,128)(2,1)} %tokens.3, bf16[128,2048]{1,0:T(8,128)(2,1)} %cot.3, ...), custom_call_target="tpu_custom_call" | custom-call | tf_op jit(solution)/shard_map/middle_kernel/pallas_call | solution.py:588
  178.6 10.3 %fusion.105 = f32[1024,1536]{0,1:T(8,128)S(1)} fusion(bf16[1024,2048]{1,0:T(8,128)(2,1)} %bitcast.180, bf16[2048,1536]{1,0:T(8,128)(2,1)} %bitcast.174), kind=kOutput, calls=%fused_computation.173 | convolution fusion | flops 6442450944 | bytes 16777216 | tf_op jit(solution)/shard_map/dot_general | solution.py:727
  188.9 6.0 %multiply_convert_fusion.2 = (bf16[1024,768]{0,1:T(8,128)(2,1)}, bf16[1024,768]{0,1:T(8,128)(2,1)}, bf16[1024,768]{0,1:T(8,128)(2,1)S(1)}) fusion(f32[1024,1536]{0,1:T(8,128)S(1)} %fusion.105, bf16[1024,2048]{1,0:T(8,128)(2,1)S(1)} %bitcast.182, bf16[768,2048]{1,0:T(8,128)(2,1)S(1)} %bitcast.186), kind=kOutput, calls=%fused_computation.24 | convolution fusion | flops 3233021952 | bytes 18350080 | tf_op jit(solution)/shard_map/dot_general | solution.py:622
  195.0 4.8 %convolution_convert_fusion.5 = bf16[768,2048]{1,0:T(8,128)(2,1)} fusion(bf16[1024,768]{0,1:T(8,128)(2,1)S(1)} %get-tuple-element.51, bf16[1024,2048]{1,0:T(8,128)(2,1)S(1)} %bitcast.183), kind=kOutput, calls=%fused_computation.20 | convolution fusion | flops 3222798336 | bytes 8912896 | tf_op jit(solution)/shard_map/dot_general | solution.py:622
  199.8 8.3 %convolution_convert_fusion.1 = bf16[1024,2048]{1,0:T(8,128)(2,1)} fusion(bf16[2048,1536]{1,0:T(8,128)(2,1)S(1)} %bitcast.177, bf16[1024,768]{0,1:T(8,128)(2,1)S(1)} %copy-done.28, bf16[1024,768]{0,1:T(8,128)(2,1)S(1)} %copy-done.27), kind=kOutput, calls=%fused_computation.16 | convolution fusion | flops 6450839552 | bytes 13631488 | tf_op jit(solution)/shard_map/dot_general | solution.py:622
  208.2 9.6 %convolution_convert_fusion = bf16[2048,1536]{1,0:T(8,128)(2,1)} fusion(bf16[1024,2048]{1,0:T(8,128)(2,1)S(1)} %bitcast.181, bf16[1024,768]{0,1:T(8,128)(2,1)S(1)} %copy-done.28, bf16[1024,768]{0,1:T(8,128)(2,1)S(1)} %copy-done.27), kind=kOutput, calls=%fused_computation.14 | convolution fusion | flops 6451888128 | bytes 13631488 | tf_op jit(solution)/shard_map/dot_general | solution.py:622
  217.8 5.3 %convolution_convert_fusion.4 = bf16[1024,2048]{1,0:T(8,128)(2,1)} fusion(bf16[1024,768]{0,1:T(8,128)(2,1)S(1)} %get-tuple-element.51, bf16[768,2048]{1,0:T(8,128)(2,1)S(1)} %bitcast.187), kind=kOutput, calls=%fused_computation.19 | convolution fusion | flops 3223322624 | bytes 8912896 | tf_op jit(solution)/shard_map/dot_general | solution.py:732
  223.0 78.4 %back_kernel.1 = (bf16[128,2048]{1,0:T(8,128)(2,1)}, f32[128,2048]{1,0:T(8,128)}, bf16[8,128,2048]{2,1,0:T(8,128)(2,1)}, bf16[8,16,1536]{2,1,0:T(8,128)(2,1)}, bf16[3,16,2048]{2,1,0:T(8,128)(2,1)}) custom-call(bf16[8,128,2048]{2,1,0:T(8,128)(2,1)} %bitcast.143, bf16[8,128,2048]{2,1,0:T(8,128)(2,1)} %bitcast.144, f32[128,2048]{1,0:T(8,128)} %get-tuple-element.38.h1, ...), custom_call_target="tpu_custom_call" | custom-call | tf_op jit(solution)/shard_map/back_kernel/pallas_call | solution.py:588
  301.4 3.6 convolution_convert_fusion.8
  305.0 2.3 convolution_convert_fusion.7
  307.3 9.2 %fusion.32 = bf16[1024,64]{0,1:T(8,128)(2,1)} fusion(bf16[1024,4,64]{0,2,1:T(8,128)(2,1)S(1)} %bitcast.147, f32[4,1024,1024]{1,2,0:T(8,128)} %get-tuple-element.84, f32[4,1024]{1,0:T(4,128)S(1)} %log_add_fusion), kind=kOutput, calls=%fused_computation.49 | convolution fusion | flops 545325056 | bytes 17448960 | tf_op jit(solution)/shard_map/gqn,qgd->nd/dot_general | solution.py:764
  316.4 0.8 slice_convert_fusion.1
  317.2 1.4 fusion.22
  318.6 0.6 fusion.19
  319.2 0.2 copy.95
  319.4 0.1 reshape.515
  319.6 1.2 copy.96
  320.8 0.1 reshape.516
  321.0 2.0 broadcast_multiply_fusion
  323.0 0.5 add.133
  323.5 14.8 %fusion = (f32[4,1024]{1,0:T(4,128)S(1)}, f32[1024,1024,4]{1,0,2:T(8,128)}) fusion(f32[4,1024,1024]{1,2,0:T(8,128)} %get-tuple-element.84, f32[4,1024]{1,0:T(4,128)S(1)} %log_add_fusion, bf16[1024,4,64]{0,2,1:T(8,128)(2,1)S(1)} %bitcast.148, f32[1024,384]{0,1:T(8,128)S(1)} %fusion.104), kind=kOutput, calls=%fused_computation.2 | convolution fusion | flops 549449728 | bytes 34242560 | tf_op jit(solution)/shard_map/qgd,nd->gqn/dot_general | solution.py:759
  338.4 0.5 slice-done.3
  338.9 8.1 %fusion.2 = bf16[4,1024,1024]{1,2,0:T(8,128)(2,1)S(1)} fusion(f32[1024,1024,4]{1,0,2:T(8,128)} %get-tuple-element.86, f32[4,1024,1024]{1,2,0:T(8,128)S(1)} %bitcast.140, f32[4,1024]{1,0:T(4,128)S(1)} %get-tuple-element.85, f32[4,1024]{1,0:T(4,128)S(1)} %log_add_fusion), kind=kLoop, calls=%fused_computation.4 | loop fusion | flops 16777216 | bytes 41975808 | tf_op jit(solution)/shard_map/convert_element_type | solution.py:761
  347.0 2.7 fusion.28
  349.7 1.6 fusion.17
  351.3 0.1 subtract_convert_fusion
  351.5 0.6 fusion.59
  352.1 3.6 convolution_convert_fusion.6
  355.8 4.4 %convolution_convert_fusion.2 = bf16[1024,2048]{1,0:T(8,128)(2,1)} fusion(bf16[2048,384]{1,0:T(8,128)(2,1)S(1)} %bitcast.189, bf16[1024,64]{0,1:T(8,128)(2,1)S(1)} %copy-done.9, bf16[1024,64]{0,1:T(8,128)(2,1)S(1)} %maximum_bitcast_fusion.1, bf16[1024,256]{0,1:T(8,128)(2,1)S(1)} %bitcast.158), kind=kOutput, calls=%fused_computation.17 | convolution fusion | flops 1615069184 | bytes 6553600 | tf_op jit(solution)/shard_map/dot_general | solution.py:622
  360.2 53.8 %end_kernel.1 = (f32[128,2048]{1,0:T(8,128)}, bf16[8,16,384]{2,1,0:T(8,128)(2,1)}, bf16[16,2048]{1,0:T(8,128)(2,1)}) custom-call(bf16[8,128,2048]{2,1,0:T(8,128)(2,1)} %bitcast.146, bf16[128,2048]{1,0:T(8,128)(2,1)} %tokens.3, f32[128,2048]{1,0:T(8,128)} %get-tuple-element.41.dh1, bf16[4,4,8,16,384]{4,3,2,1,0:T(8,128)(2,1)} %bitcast.150, ...), custom_call_target="tpu_custom_call" | custom-call | tf_op jit(solution)/shard_map/end_kernel/pallas_call | solution.py:588
  413.9 1.5 convert_element_type.180
  415.5 0.9 convert_element_type.179
  416.4 0.8 broadcast_multiply_fusion.2
  417.6 0.8 broadcast_multiply_fusion.3
  418.4 0.5 add_add_fusion
  418.9 0.8 copy.108
  419.7 2.3 copy.109
  (101 shorter events, 1.1 us)
Async XLA Ops:
  0.6 14.3 %copy-start = (bf16[128,2048]{1,0:T(8,128)(2,1)S(1)}, bf16[128,2048]{1,0:T(8,128)(2,1)}, u32[]{:S(2)}) copy-start(bf16[128,2048]{1,0:T(8,128)(2,1)} %tokens.3) | copy-start | bytes 1572868
  1.4 11.6 %copy-start.18 = (f32[16]{0:T(128)}, f32[16]{0:T(128)S(1)}, u32[]{:S(2)}) copy-start(f32[16]{0:T(128)S(1)} %convert_element_type.146) | copy-start | bytes 196
  66.9 8.1 %copy-start.10 = (bf16[1024,32]{0,1:T(8,128)(2,1)}, bf16[1024,32]{0,1:T(8,128)(2,1)S(1)}, u32[]{:S(2)}) copy-start(bf16[1024,32]{0,1:T(8,128)(2,1)S(1)} %get-tuple-element.62) | copy-start | bytes 196612
  66.9 8.1 %copy-start.12 = (bf16[1024,32]{0,1:T(8,128)(2,1)}, bf16[1024,32]{0,1:T(8,128)(2,1)S(1)}, u32[]{:S(2)}) copy-start(bf16[1024,32]{0,1:T(8,128)(2,1)S(1)} %get-tuple-element.63) | copy-start | bytes 196612
  67.1 7.8 %copy-start.1 = (bf16[1024,4,32]{0,2,1:T(8,128)(2,1)}, bf16[1024,4,32]{0,2,1:T(8,128)(2,1)S(1)}, u32[]{:S(2)}) copy-start(bf16[1024,4,32]{0,2,1:T(8,128)(2,1)S(1)} %get-tuple-element.54) | copy-start | bytes 786436
  67.1 7.8 %copy-start.3 = (bf16[1024,4,32]{0,2,1:T(8,128)(2,1)}, bf16[1024,4,32]{0,2,1:T(8,128)(2,1)S(1)}, u32[]{:S(2)}) copy-start(bf16[1024,4,32]{0,2,1:T(8,128)(2,1)S(1)} %get-tuple-element.55) | copy-start | bytes 786436
  83.0 7.5 %copy-start.5 = (bf16[4,4,16,2048]{3,2,1,0:T(8,128)(2,1)S(1)}, bf16[4,4,16,2048]{3,2,1,0:T(8,128)(2,1)}, u32[]{:S(2)}) copy-start(bf16[4,4,16,2048]{3,2,1,0:T(8,128)(2,1)} %get-tuple-element.31) | copy-start | bytes 3145732
  178.6 10.3 %copy-start.22 = (bf16[8,128,2048]{2,1,0:T(8,128)(2,1)S(1)}, bf16[8,128,2048]{2,1,0:T(8,128)(2,1)}, u32[]{:S(2)}) copy-start(bf16[8,128,2048]{2,1,0:T(8,128)(2,1)} %get-tuple-element.34) | copy-start | bytes 12582916
  178.6 10.3 %copy-start.24 = (bf16[4,4,3,16,2048]{4,3,2,1,0:T(8,128)(2,1)S(1)}, bf16[4,4,3,16,2048]{4,3,2,1,0:T(8,128)(2,1)}, u32[]{:S(2)}) copy-start(bf16[4,4,3,16,2048]{4,3,2,1,0:T(8,128)(2,1)} %get-tuple-element.35) | copy-start | bytes 9437188
  178.6 21.2 %slice-start.4 = ((s8[6291456]{0:T(1024)(128)(4,1)}), s8[2097152]{0:T(1024)(128)(4,1)S(1)}, s32[]{:S(2)}) async-start(s8[6291456]{0:T(1024)(128)(4,1)} %bitcast.175), calls=%async_computation.4 | async-start | bytes 4194304
  188.9 10.9 %slice-start.5 = ((s8[6291456]{0:T(1024)(128)(4,1)}), s8[4194304]{0:T(1024)(128)(4,1)S(1)}, s32[]{:S(2)}) async-start(s8[6291456]{0:T(1024)(128)(4,1)} %bitcast.175), calls=%async_computation.5 | async-start | bytes 8388608
  195.0 4.8 %copy-start.27 = (bf16[1024,768]{0,1:T(8,128)(2,1)S(1)}, bf16[1024,768]{0,1:T(8,128)(2,1)}, u32[]{:S(2)}) copy-start(bf16[1024,768]{0,1:T(8,128)(2,1)} %get-tuple-element.49) | copy-start | bytes 4718596
  195.0 4.8 %copy-start.28 = (bf16[1024,768]{0,1:T(8,128)(2,1)S(1)}, bf16[1024,768]{0,1:T(8,128)(2,1)}, u32[]{:S(2)}) copy-start(bf16[1024,768]{0,1:T(8,128)(2,1)} %get-tuple-element.50) | copy-start | bytes 4718596
  199.8 8.3 %copy-start.21 = (bf16[8,128,2048]{2,1,0:T(8,128)(2,1)S(1)}, bf16[8,128,2048]{2,1,0:T(8,128)(2,1)}, u32[]{:S(2)}) copy-start(bf16[8,128,2048]{2,1,0:T(8,128)(2,1)} %get-tuple-element.36) | copy-start | bytes 12582916
  301.4 3.6 copy-start.23
  307.3 9.2 %copy-start.15 = (bf16[3,16,2048]{2,1,0:T(8,128)(2,1)S(1)}, bf16[3,16,2048]{2,1,0:T(8,128)(2,1)}, u32[]{:S(2)}) copy-start(bf16[3,16,2048]{2,1,0:T(8,128)(2,1)} %get-tuple-element.46) | copy-start | bytes 589828
  307.3 9.9 %copy-start.26 = (bf16[8,16,1536]{2,1,0:T(8,128)(2,1)S(1)}, bf16[8,16,1536]{2,1,0:T(8,128)(2,1)}, u32[]{:S(2)}) copy-start(bf16[8,16,1536]{2,1,0:T(8,128)(2,1)} %get-tuple-element.45) | copy-start | bytes 1179652
  316.4 4.5 %copy-start.6 = (bf16[16,5632]{1,0:T(8,128)(2,1)S(1)}, bf16[16,5632]{1,0:T(8,128)(2,1)}, u32[]{:S(2)}) copy-start(bf16[16,5632]{1,0:T(8,128)(2,1)} %param.23) | copy-start | bytes 540676
  323.0 15.4 %slice-start = ((s8[16777216]{0:T(1024)(128)(4,1)}), s8[4194304]{0:T(1024)(128)(4,1)S(1)}, s32[]{:S(2)}) async-start(s8[16777216]{0:T(1024)(128)(4,1)} %bitcast.139), calls=%async_computation | async-start | bytes 8388608
  323.5 14.9 %slice-start.1 = ((s8[16777216]{0:T(1024)(128)(4,1)}), s8[4194304]{0:T(1024)(128)(4,1)S(1)}, s32[]{:S(2)}) async-start(s8[16777216]{0:T(1024)(128)(4,1)} %bitcast.139), calls=%async_computation.1 | async-start | bytes 8388608
  323.5 14.9 %slice-start.2 = ((s8[16777216]{0:T(1024)(128)(4,1)}), s8[4194304]{0:T(1024)(128)(4,1)S(1)}, s32[]{:S(2)}) async-start(s8[16777216]{0:T(1024)(128)(4,1)} %bitcast.139), calls=%async_computation.2 | async-start | bytes 8388608
  323.5 15.3 %slice-start.3 = ((s8[16777216]{0:T(1024)(128)(4,1)}), s8[4194304]{0:T(1024)(128)(4,1)S(1)}, s32[]{:S(2)}) async-start(s8[16777216]{0:T(1024)(128)(4,1)} %bitcast.139), calls=%async_computation.3 | async-start | bytes 8388608
  338.9 8.1 %copy-start.2 = (bf16[1024,4,32]{0,2,1:T(8,128)(2,1)S(1)}, bf16[1024,4,32]{0,2,1:T(8,128)(2,1)}, u32[]{:S(2)}) copy-start(bf16[1024,4,32]{0,2,1:T(8,128)(2,1)} %copy-done.1) | copy-start | bytes 786436
  338.9 8.1 %copy-start.4 = (bf16[1024,4,32]{0,2,1:T(8,128)(2,1)S(1)}, bf16[1024,4,32]{0,2,1:T(8,128)(2,1)}, u32[]{:S(2)}) copy-start(bf16[1024,4,32]{0,2,1:T(8,128)(2,1)} %copy-done.3) | copy-start | bytes 786436
  347.0 2.7 copy-start.11
  347.0 2.7 copy-start.13
  349.7 1.6 copy-start.7
  349.7 2.4 copy-start.9
  349.7 2.4 copy-start.20
  352.1 3.6 copy-start.25
  360.2 56.3 %copy-start.14 = (bf16[16,2048]{1,0:T(8,128)(2,1)S(1)}, bf16[16,2048]{1,0:T(8,128)(2,1)}, u32[]{:S(2)}) copy-start(bf16[16,2048]{1,0:T(8,128)(2,1)} %param.18) | copy-start | bytes 196612
  360.2 56.3 %copy-start.19 = (f32[16]{0:T(128)S(1)}, f32[16]{0:T(128)}, u32[]{:S(2)}) copy-start(f32[16]{0:T(128)} %copy-done.18) | copy-start | bytes 196
  360.2 57.4 %copy-start.16 = (bf16[16,256]{1,0:T(8,128)(2,1)S(1)}, bf16[16,256]{1,0:T(8,128)(2,1)}, u32[]{:S(2)}) copy-start(bf16[16,256]{1,0:T(8,128)(2,1)} %param.19) | copy-start | bytes 24580
  360.2 57.4 %copy-start.17 = (bf16[16,256]{1,0:T(8,128)(2,1)S(1)}, bf16[16,256]{1,0:T(8,128)(2,1)}, u32[]{:S(2)}) copy-start(bf16[16,256]{1,0:T(8,128)(2,1)} %param.20) | copy-start | bytes 24580
  360.2 58.7 %copy-start.8 = (bf16[128,2048]{1,0:T(8,128)(2,1)S(1)}, bf16[128,2048]{1,0:T(8,128)(2,1)}, u32[]{:S(2)}) copy-start(bf16[128,2048]{1,0:T(8,128)(2,1)} %get-tuple-element.98) | copy-start | bytes 1572868
